TPU v7x, 32 devices: a whole 2x2x4 slice. The times are simulated.
32 devices in a mesh: row: 4 (over x, core), col: 8 (over z, y).
Axes of the slice: x: 2, y: 2, z: 4, core: 2. Of those that a mesh axis runs over, the one named last changes fastest.
Arguments:
- t_slab: bfloat16 [4, 2, 512, 64], P('row', None, 'col'), may hold values from -6 to 6
- w_cycle: bfloat16 [128, 16384], P('row', 'col'), may hold values from -0.5 to 0.5
Outputs:
- t_amp: bfloat16 [2048, 128], P('row', 'col')
- cycle_z: float32 [2048, 16384], P('row', 'col')
All inputs are finite; a program needn't handle non-finite values.
Results may differ from a plain program's by a relative error of at most 0.001.
Values may be sent and summed in bfloat16 or wider, within the bound.
A program may use at most 64 MiB of HBM per device.

v0:
```python
import jax
import jax.numpy as jnp
from jax import lax
from jax.sharding import PartitionSpec as P


def shards(t_slab, w_cycle):
    local_rows = jnp.transpose(t_slab[0], (1, 0, 2)).reshape(
        t_slab.shape[2], t_slab.shape[1] * t_slab.shape[3]
    )
    t_tile = lax.all_to_all(local_rows, "col", split_axis=1, concat_axis=0, tiled=True)
    t_full = lax.all_gather(t_tile, "col", axis=1, tiled=True)
    w_full = lax.all_gather(w_cycle, "row", axis=0, tiled=True)
    cycle_z = jnp.dot(t_full, w_full, preferred_element_type=jnp.float32)
    return (t_tile, cycle_z)


def solution(mesh):
    placed = (P("row", None, "col", None), P("row", "col"))
    return jax.shard_map(
        shards,
        mesh=mesh,
        in_specs=placed,
        out_specs=(P("row", "col"), P("row", "col")),
        check_vma=False,
    )
```

profile of v0, /device:TPU:0, one launch (start us, length us, event | category | flops | bytes accessed | tf_op | source)
XLA Modules:
  0.0 50.9 jit_solution(17427372366816520272)
XLA Ops:
  0.6 0.8 %copy.5 = bf16[1,2,64,64]{2,3,1,0:T(8,128)(2,1)S(1)} copy(bf16[1,2,64,64]{3,2,1,0:T(8,128)(2,1)} %param.2) | data formatting | bytes 32768 | tf_op args[0]
  1.5 0.7 %reshape.9 = bf16[8,2,512]{2,1,0:T(2,128)(2,1)} reshape(bf16[8,16,64]{2,1,0:T(8,128)(2,1)S(1)} %bitcast.14) | data formatting | bytes 32768
  2.2 7.3 %all-to-all-start = ((bf16[8,2,512]{2,1,0:T(2,128)(2,1)}), bf16[8,2,512]{2,1,0:T(2,128)(2,1)S(1)}, u32[]{:S(2)}, u32[]{:S(2)}) async-start(bf16[8,2,512]{2,1,0:T(2,128)(2,1)} %reshape.9), calls=%async_computation | async-start | bytes 32768 | tf_op jit(solution)/shard_map/all_to_all | solution.py:11
  9.5 7.4 %all_gather.7 = bf16[128,2048]{1,0:T(8,128)(2,1)S(1)} all-gather(bf16[32,2048]{1,0:T(8,128)(2,1)} %param.3), channel_id=1, replica_groups=mesh['row'=4,'col'=8] {'row'}, dimensions={0}, use_global_device_ids=true | all-gather | bytes 655360 | tf_op jit(solution)/shard_map/all_gather | solution.py:13
  16.8 0.0 all-to-all-done
  16.8 0.1 reshape.10
  17.0 0.1 all_to_all.17
  17.1 0.0 copy-start
  17.1 31.1 %all_gather.6 = bf16[512,128]{0,1:T(8,128)(2,1)S(1)} all-gather(bf16[512,16]{0,1:T(8,128)(2,1)S(1)} %all_to_all.17), channel_id=1, replica_groups=mesh['row'=4,'col'=8] {'col'}, dimensions={1}, use_global_device_ids=true | all-gather | bytes 147456 | tf_op jit(solution)/shard_map/all_gather | solution.py:12
  48.2 2.7 %fusion = f32[512,2048]{1,0:T(8,128)} fusion(bf16[512,128]{0,1:T(8,128)(2,1)S(1)} %all_gather.6, bf16[128,2048]{1,0:T(8,128)(2,1)S(1)} %all_gather.7), kind=kOutput, calls=%fused_computation.1 | convolution fusion | flops 268435456 | bytes 4849664 | tf_op jit(solution)/shard_map/dot_general | solution.py:14
  50.9 0.0 copy-done
  (2 shorter events, 0.0 us)
Async XLA Ops:
  2.2 14.7 %all-to-all-start = ((bf16[8,2,512]{2,1,0:T(2,128)(2,1)}), bf16[8,2,512]{2,1,0:T(2,128)(2,1)S(1)}, u32[]{:S(2)}, u32[]{:S(2)}) async-start(bf16[8,2,512]{2,1,0:T(2,128)(2,1)} %reshape.9), calls=%async_computation | async-start | bytes 32768 | tf_op jit(solution)/shard_map/all_to_all | solution.py:11
  17.1 33.8 %copy-start = (bf16[512,16]{0,1:T(8,128)(2,1)}, bf16[512,16]{0,1:T(8,128)(2,1)S(1)}, u32[]{:S(2)}) copy-start(bf16[512,16]{0,1:T(8,128)(2,1)S(1)} %all_to_all.17) | copy-start | bytes 49156
where the time goes:
time: 51.2 us; the launch traced here: 50.9 us
  blocking collectives  38.4 us (75%)
  starting transfers between devices  7.28 us (14%)
  matrix products  2.74 us (5%)
  local copies, waits for them, and re-layouts  1.77 us (3%)
  between operations  0.66 us (1%)
    all_gather x1, blocking collectives, shards(): t_full = lax.all_gather(t_tile, 'col', axis=1, tiled=True)  31.1 us
    all_gather x1, blocking collectives, shards(): w_full = lax.all_gather(w_cycle, 'row', axis=0, tiled=True)  7.37 us
    all_to_all x1, starting transfers between devices, shards(): lax.all_to_all(local_rows, 'col', split_axis=1, concat_axis=0, tiled=True)  7.28 us
    dot_general x1, matrix products, shards(): cycle_z = jnp.dot(t_full, w_full, preferred_element_type=jnp.float32)  2.74 us
    unnamed x5, local copies, waits for them, and re-layouts  1.65 us
  transfers between devices with their start and end apart: 1, of which 0 were waited for; matrix products, arithmetic and copies ran while one was open for 0% of the time, Pallas kernels for 0%

commit v1 on v0

--- a/solution.py
+++ b/solution.py
@@ -9,7 +9,14 @@
         t_slab.shape[2], t_slab.shape[1] * t_slab.shape[3]
     )
     t_tile = lax.all_to_all(local_rows, "col", split_axis=1, concat_axis=0, tiled=True)
-    t_full = lax.all_gather(t_tile, "col", axis=1, tiled=True)
+    ways, here = (lax.axis_size("col"), lax.axis_index("col"))
+    t_full, reach = (t_tile, 1)
+    while reach < ways:
+        theirs = lax.ppermute(t_full, "col", [(d, d ^ reach) for d in range(ways)])
+        mine_first = jnp.concatenate([t_full, theirs], axis=1)
+        theirs_first = jnp.concatenate([theirs, t_full], axis=1)
+        t_full = jnp.where(here & reach == 0, mine_first, theirs_first)
+        reach = 2 * reach
     w_full = lax.all_gather(w_cycle, "row", axis=0, tiled=True)
     cycle_z = jnp.dot(t_full, w_full, preferred_element_type=jnp.float32)
     return (t_tile, cycle_z)

time: 51.2 us -> 34.6 us (0.68)
  blocking collectives: 38.4 us -> 21 us
  waiting for transfers between devices: 0.01 us -> 6.95 us
  starting transfers between devices: 7.28 us -> 1.79 us
  local copies, waits for them, and re-layouts: 1.77 us -> 1.16 us
    all_gather x1 -> x0, blocking collectives: 31.1 us -> none  [shards(): t_full = lax.all_gather(t_tile, 'col', axis=1, tiled=True)]
    all_to_all x0 -> x1, blocking collectives: none -> 13.7 us  [shards(): lax.all_to_all(local_rows, 'col', split_axis=1, concat_axis=0, tiled=True)]
    all_to_all x1 -> x0, starting transfers between devices: 7.28 us -> none  [shards(): lax.all_to_all(local_rows, 'col', split_axis=1, concat_axis=0, tiled=True)]
    ppermute x0 -> x3, waiting for transfers between devices: none -> 6.95 us  [shards(): theirs = lax.ppermute(t_full, 'col', [(d, d ^ reach) for d in range(ways)])]
    ppermute x0 -> x3, starting transfers between devices: none -> 1.79 us  [shards(): theirs = lax.ppermute(t_full, 'col', [(d, d ^ reach) for d in range(ways)])]
    unnamed x5, local copies, waits for them, and re-layouts: 1.65 us -> 1.04 us
  transfers between devices with their start and end apart: 1 -> 3, of which waited for: 0 -> 2; matrix products, arithmetic and copies ran while one was open for 0% -> 0% of each run, Pallas kernels for 0% -> 0%
where the time goes in v1:
time: 34.6 us; the launch traced here: 34.4 us
  blocking collectives  21 us (61%)
  waiting for transfers between devices  6.95 us (20%)
  matrix products  2.75 us (8%)
  starting transfers between devices  1.79 us (5%)
  local copies, waits for them, and re-layouts  1.16 us (3%)
  between operations  0.67 us (2%)
    all_to_all x1, blocking collectives, shards(): lax.all_to_all(local_rows, 'col', split_axis=1, concat_axis=0, tiled=True)  13.7 us
    all_gather x1, blocking collectives, shards(): w_full = lax.all_gather(w_cycle, 'row', axis=0, tiled=True)  7.37 us
    ppermute x3, waiting for transfers between devices, shards(): theirs = lax.ppermute(t_full, 'col', [(d, d ^ reach) for d in range(ways)])  6.95 us
    dot_general x1, matrix products, shards(): cycle_z = jnp.dot(t_full, w_full, preferred_element_type=jnp.float32)  2.75 us
    ppermute x3, starting transfers between devices, shards(): theirs = lax.ppermute(t_full, 'col', [(d, d ^ reach) for d in range(ways)])  1.79 us
    unnamed x5, local copies, waits for them, and re-layouts  1.04 us
  transfers between devices with their start and end apart: 3, of which 2 were waited for; matrix products, arithmetic and copies ran while one was open for 0% of the time, Pallas kernels for 0%

profile of v1, /device:TPU:0, one launch (start us, length us, event | category | flops | bytes accessed | tf_op | source)
XLA Modules:
  0.0 34.4 jit_solution(5344128521617647981)
XLA Ops:
  0.6 0.8 %copy.5 = bf16[1,2,64,64]{2,3,1,0:T(8,128)(2,1)S(1)} copy(bf16[1,2,64,64]{3,2,1,0:T(8,128)(2,1)} %param.2) | data formatting | bytes 32768 | tf_op args[0]
  1.5 0.1 reshape.9
  1.6 13.7 %all_to_all.19 = bf16[8,2,512]{2,1,0:T(2,128)(2,1)S(1)} all-to-all(bf16[8,2,512]{2,1,0:T(2,128)(2,1)S(1)} %reshape.9), channel_id=1, replica_groups=mesh['row'=4,'col'=8] {'col'}, dimensions={0} | all-to-all | bytes 32768 | tf_op jit(solution)/shard_map/all_to_all | solution.py:11
  15.2 0.1 reshape.10
  15.4 0.1 all_to_all.17
  15.5 0.0 copy-start
  15.5 0.6 %collective-permute-start = (bf16[512,16]{0,1:T(8,128)(2,1)S(1)}, bf16[512,16]{0,1:T(8,128)(2,1)S(1)}, u32[]{:S(2)}, u32[]{:S(2)}) collective-permute-start(bf16[512,16]{0,1:T(8,128)(2,1)S(1)} %all_to_all.17), channel_id=1, source_target_pairs={{0,1},{1,0},{2,3},{3,2},{4,5},{5,4},{6,7},{7,6},{8,9},{9,8},{10,11... | collective-permute-start | bytes 49160 | tf_op jit(solution)/shard_map/ppermute | solution.py:15
  16.1 3.2 %collective-permute-done = bf16[512,16]{0,1:T(8,128)(2,1)S(1)} collective-permute-done((bf16[512,16]{0,1:T(8,128)(2,1)S(1)}, bf16[512,16]{0,1:T(8,128)(2,1)S(1)}, u32[]{:S(2)}, u32[]{:S(2)}) %collective-permute-start) | collective-permute-done | bytes 16416 | tf_op jit(solution)/shard_map/ppermute | solution.py:15
  19.3 0.5 %collective-permute-start.1 = (bf16[512,32]{0,1:T(8,128)(2,1)S(1)}, bf16[512,32]{0,1:T(8,128)(2,1)S(1)}, u32[]{:S(2)}, u32[]{:S(2)}) collective-permute-start(bf16[512,32]{0,1:T(8,128)(2,1)S(1)} %maximum_select_fusion.3), channel_id=1, source_target_pairs={{0,2},{1,3},{2,0},{3,1},{4,6},{5,7},{6,4},{7,5},{8,10},{9,11},{10,... | collective-permute-start | bytes 98312 | tf_op jit(solution)/shard_map/ppermute | solution.py:15
  19.8 3.7 %collective-permute-done.1 = bf16[512,32]{0,1:T(8,128)(2,1)S(1)} collective-permute-done((bf16[512,32]{0,1:T(8,128)(2,1)S(1)}, bf16[512,32]{0,1:T(8,128)(2,1)S(1)}, u32[]{:S(2)}, u32[]{:S(2)}) %collective-permute-start.1) | collective-permute-done | bytes 32800 | tf_op jit(solution)/shard_map/ppermute | solution.py:15
  23.6 0.7 %collective-permute-start.2 = (bf16[512,64]{0,1:T(8,128)(2,1)S(1)}, bf16[512,64]{0,1:T(8,128)(2,1)S(1)}, u32[]{:S(2)}, u32[]{:S(2)}) collective-permute-start(bf16[512,64]{0,1:T(8,128)(2,1)S(1)} %maximum_select_fusion.2), channel_id=1, source_target_pairs={{0,4},{1,5},{2,6},{3,7},{4,0},{5,1},{6,2},{7,3},{8,12},{9,13},{10,... | collective-permute-start | bytes 196616 | tf_op jit(solution)/shard_map/ppermute | solution.py:15
  24.2 7.4 %all_gather.3 = bf16[128,2048]{1,0:T(8,128)(2,1)S(1)} all-gather(bf16[32,2048]{1,0:T(8,128)(2,1)} %param.3), channel_id=1, replica_groups=mesh['row'=4,'col'=8] {'row'}, dimensions={0}, use_global_device_ids=true | all-gather | bytes 655360 | tf_op jit(solution)/shard_map/all_gather | solution.py:20
  31.6 0.0 collective-permute-done.2
  31.6 2.7 %fusion = f32[512,2048]{1,0:T(8,128)} fusion(bf16[128,2048]{1,0:T(8,128)(2,1)S(1)} %all_gather.3, bf16[512,64]{0,1:T(8,128)(2,1)S(1)} %collective-permute-done.2, bf16[512,64]{0,1:T(8,128)(2,1)S(1)} %maximum_select_fusion.2, pred[]{:T(512)S(6)} %eq.9), kind=kOutput, calls=%fused_computation.1 | convolution fusion | flops 269025280 | bytes 4849665 | tf_op jit(solution)/shard_map/dot_general | solution.py:21
  34.4 0.0 copy-done
  (4 shorter events, 0.0 us)
Async XLA Ops:
  15.5 18.9 %copy-start = (bf16[512,16]{0,1:T(8,128)(2,1)}, bf16[512,16]{0,1:T(8,128)(2,1)S(1)}, u32[]{:S(2)}) copy-start(bf16[512,16]{0,1:T(8,128)(2,1)S(1)} %all_to_all.17) | copy-start | bytes 49156
  15.5 3.8 %collective-permute-start = (bf16[512,16]{0,1:T(8,128)(2,1)S(1)}, bf16[512,16]{0,1:T(8,128)(2,1)S(1)}, u32[]{:S(2)}, u32[]{:S(2)}) collective-permute-start(bf16[512,16]{0,1:T(8,128)(2,1)S(1)} %all_to_all.17), channel_id=1, source_target_pairs={{0,1},{1,0},{2,3},{3,2},{4,5},{5,4},{6,7},{7,6},{8,9},{9,8},{10,11... | collective-permute-start | bytes 49160 | tf_op jit(solution)/shard_map/ppermute | solution.py:15
  19.3 4.3 %collective-permute-start.1 = (bf16[512,32]{0,1:T(8,128)(2,1)S(1)}, bf16[512,32]{0,1:T(8,128)(2,1)S(1)}, u32[]{:S(2)}, u32[]{:S(2)}) collective-permute-start(bf16[512,32]{0,1:T(8,128)(2,1)S(1)} %maximum_select_fusion.3), channel_id=1, source_target_pairs={{0,2},{1,3},{2,0},{3,1},{4,6},{5,7},{6,4},{7,5},{8,10},{9,11},{10,... | collective-permute-start | bytes 98312 | tf_op jit(solution)/shard_map/ppermute | solution.py:15
  23.6 8.0 %collective-permute-start.2 = (bf16[512,64]{0,1:T(8,128)(2,1)S(1)}, bf16[512,64]{0,1:T(8,128)(2,1)S(1)}, u32[]{:S(2)}, u32[]{:S(2)}) collective-permute-start(bf16[512,64]{0,1:T(8,128)(2,1)S(1)} %maximum_select_fusion.2), channel_id=1, source_target_pairs={{0,4},{1,5},{2,6},{3,7},{4,0},{5,1},{6,2},{7,3},{8,12},{9,13},{10,... | collective-permute-start | bytes 196616 | tf_op jit(solution)/shard_map/ppermute | solution.py:15
